TPU v7x, 32 devices: a whole 2x2x4 slice. The times are simulated.
32 devices in a mesh: sec: 4 (over z), dev: 8 (over y, x, core).
Axes of the slice: x: 2, y: 2, z: 4, core: 2. Of those that a mesh axis runs over, the one named last changes fastest.
Arguments:
- x_input: bfloat16 [65536, 2048], P(('sec', 'dev'))
- log_decay: float32 [65536, 32], P(('sec', 'dev')), as said below
- b_input: bfloat16 [65536, 64], P(('sec', 'dev')), may hold values from -6 to 6
- c_input: bfloat16 [65536, 64], P(('sec', 'dev')), may hold values from -0.75 to 0.75
- skip_gain: float32 [32], replicated, may hold values from 0.5 to 2
- score_weight: bfloat16 [2048], replicated, may hold values from -0.125 to 0.125
- trace_lengths: int32 [4], replicated, may hold values from 1 to 32768, 65536 in all
- step_lengths: int32 [512], replicated, may hold values from 1 to 512, 65536 in all
- step_slot: int32 [512], replicated, may hold values from 0 to 511, each once
Outputs:
- y_output: bfloat16 [65536, 2048], P(('sec', 'dev'))
- step_scores: float32 [512], P(('sec', 'dev'))
Inputs may be any that keep to these rules, and one draw needn't show every extreme that they name: `trace_lengths`: the lengths sum to 65536; one trace has exactly 32768 tokens. `step_lengths`: the lengths sum to 65536; some step has exactly 512 tokens. `step_slot`: each slot is named by exactly one step. `log_decay`: every entry is negative.
All inputs are finite; a program needn't handle non-finite values.
Results may differ from a plain program's by a relative error of at most 0.0053.
Values sent between devices are 32-bit elements; how exact they have to be, the bound alone decides.
A program may use at most 384 MiB of HBM per device.

v0:
```python
import jax
import jax.numpy as jnp
from jax import lax
from jax.sharding import PartitionSpec as P

GROUP = 256


def entering(part, axis, combine, identity):
    place = lax.axis_index(axis)
    gathered = jax.tree.map(lambda a: lax.all_gather(a, axis), part)
    state = jax.tree.map(lambda a, e: jnp.zeros_like(a) + jnp.asarray(e, a.dtype), part, identity)

    def one(turn, state):
        return combine(
            state, jax.tree.map(lambda a: lax.dynamic_index_in_dim(a, turn, 0, False), gathered)
        )

    return lax.fori_loop(0, place, one, state)


def from_root(value, axis, root):
    mine = lax.axis_index(axis) == root
    return lax.psum(jnp.where(mine, value, jnp.zeros_like(value)), axis)


def trace_ids(starts, positions):
    return jnp.sum((starts[None, :] <= positions[:, None]).astype(jnp.int32), axis=1)


def combine(early, late):
    return (early[0] * late[0], late[0][:, None, None] * early[1] + late[1])


def shards(
    x_input,
    log_decay,
    b_input,
    c_input,
    skip_gain,
    score_weight,
    trace_lengths,
    step_lengths,
    step_slot,
):
    rows = x_input.shape[0]
    heads = log_decay.shape[1]
    width = x_input.shape[1]
    head_size = width // heads
    state_size = b_input.shape[1]
    count = rows // GROUP
    index = lax.axis_index(("sec", "dev"))
    base = index * rows
    starts = jnp.cumsum(trace_lengths) - trace_lengths
    positions = base + jnp.arange(rows, dtype=jnp.int32)
    trace = trace_ids(starts, positions).reshape(count, GROUP)
    prev = trace_ids(starts, base + jnp.arange(count, dtype=jnp.int32) * GROUP - 1)
    x_blocks = x_input.reshape(count, GROUP, heads, head_size)
    c_blocks = c_input.reshape(count, GROUP, state_size)
    inputs = (
        x_blocks,
        log_decay.reshape(count, GROUP, heads),
        b_input.reshape(count, GROUP, state_size),
        c_blocks,
        trace,
        prev,
    )
    order = jnp.arange(GROUP, dtype=jnp.int32)
    causal = order[:, None] >= order[None, :]
    lower_ones = causal.astype(jnp.float32)

    def local_block(held, item):
        state_local, factor_prod = held
        x_heads, decay_group, b_group, c_group, trace_group, prev_trace = item
        cum = jnp.dot(
            lower_ones,
            decay_group,
            precision=lax.Precision.HIGHEST,
            preferred_element_type=jnp.float32,
        )
        cum_heads = cum.T
        keep = causal & (trace_group[:, None] == trace_group[None, :])
        gram = jnp.dot(c_group, b_group.T, preferred_element_type=jnp.float32)
        diff = cum_heads[:, :, None] - cum_heads[:, None, :]
        weight = (gram[None] * jnp.exp(jnp.where(keep[None], diff, -jnp.inf))).astype(jnp.bfloat16)
        intra = jnp.einsum("hts,shp->thp", weight, x_heads, preferred_element_type=jnp.float32)
        to_end = (
            jnp.exp(cum[-1][None, :] - cum)
            * (trace_group == trace_group[-1]).astype(jnp.float32)[:, None]
        )
        scaled = (x_heads.astype(jnp.float32) * to_end[:, :, None]).astype(jnp.bfloat16)
        new_state = jnp.einsum("shp,sn->hpn", scaled, b_group, preferred_element_type=jnp.float32)
        carry = jnp.exp(cum) * (trace_group == prev_trace).astype(jnp.float32)[:, None]
        factor = carry[-1]
        following = (factor[:, None, None] * state_local + new_state, factor_prod * factor)
        return (following, (intra, state_local, factor_prod, carry))

    start_held = (
        jnp.zeros((heads, head_size, state_size), jnp.float32),
        jnp.ones((heads,), jnp.float32),
    )
    (state_end, factor_end), (intra, state_enter, factor_enter, carry) = lax.scan(
        local_block, start_held, inputs
    )
    own = (factor_end, state_end)
    identity = (
        jnp.ones((heads,), jnp.float32),
        jnp.zeros((heads, head_size, state_size), jnp.float32),
    )
    within = entering(own, "dev", combine, identity)
    whole = combine(within, own)
    total = (
        from_root(whole[0], "dev", lax.axis_size("dev") - 1),
        from_root(whole[1], "dev", lax.axis_size("dev") - 1),
    )
    across = entering(total, "sec", combine, identity)
    incoming = combine(across, within)
    state_in = incoming[1]
    full_state = (factor_enter[:, :, None, None] * state_in[None] + state_enter).astype(
        jnp.bfloat16
    )
    inter = (
        jnp.einsum("ktn,khpn->kthp", c_blocks, full_state, preferred_element_type=jnp.float32)
        * carry[..., None]
    )
    mixed = intra + inter + skip_gain[None, None, :, None] * x_blocks.astype(jnp.float32)
    y_output = mixed.astype(jnp.bfloat16).reshape(rows, width)
    score = jnp.dot(y_output, score_weight, preferred_element_type=jnp.float32)
    total_steps = step_slot.shape[0]
    step_starts = jnp.cumsum(step_lengths) - step_lengths
    step_ends = step_starts + step_lengths
    inside = (step_starts[None, :] <= positions[:, None]) & (
        positions[:, None] < step_ends[None, :]
    )
    token_slot = jnp.sum(jnp.where(inside, step_slot[None, :], 0), axis=1)
    column_block = min(512, total_steps)
    pieces = []
    for first_column in range(0, total_steps, column_block):
        span = min(column_block, total_steps - first_column)
        column_ids = first_column + jnp.arange(span, dtype=jnp.int32)
        table = (token_slot[:, None] == column_ids[None, :]).astype(jnp.float32)
        pieces.append(
            jnp.dot(
                score[None, :],
                table,
                precision=lax.Precision.HIGHEST,
                preferred_element_type=jnp.float32,
            )[0]
        )
    spread = jnp.concatenate(pieces, axis=0)
    devices = lax.axis_size(("sec", "dev"))
    owned = total_steps // devices
    sums = lax.psum_scatter(spread, ("sec", "dev"), scatter_dimension=0, tiled=True)
    own_slots = index * owned + jnp.arange(owned, dtype=jnp.int32)
    own_lengths = jnp.sum(
        jnp.where(step_slot[None, :] == own_slots[:, None], step_lengths[None, :], 0), axis=1
    )
    step_scores = sums / own_lengths.astype(jnp.float32)
    return (y_output, step_scores)


def solution(mesh):
    placed = (
        P(("sec", "dev"), None),
        P(("sec", "dev"), None),
        P(("sec", "dev"), None),
        P(("sec", "dev"), None),
        P(),
        P(),
        P(),
        P(),
        P(),
    )
    return jax.shard_map(
        shards,
        mesh=mesh,
        in_specs=placed,
        out_specs=(P(("sec", "dev"), None), P(("sec", "dev"))),
        check_vma=False,
    )
```

profile of v0, /device:TPU:0, one launch (start us, length us, event | category | flops | bytes accessed | tf_op | source)
XLA Modules:
  0.0 459.2 jit_solution(5551058934958775714)
XLA Ops:
  9.0 24.4 %reshape.186 = bf16[8,256,32,64]{3,2,1,0:T(8,128)(2,1)} reshape(bf16[2048,2048]{1,0:T(8,128)(2,1)} %param.15) | data formatting | bytes 16777216 | tf_op jit(solution)/shard_map/reshape | solution.py:58
  33.4 19.5 %copy.35 = bf16[8,256,32,64]{1,3,2,0:T(8,128)(2,1)} copy(bf16[8,256,32,64]{3,2,1,0:T(8,128)(2,1)} %reshape.186) | data formatting | bytes 16777216
  54.5 86.5 %while.47 = (s32[]{:T(128)}, f32[32,64,64]{2,1,0:T(8,128)S(1)}, f32[32]{0:T(128)S(1)}, f32[8,256,32,64]{1,3,2,0:T(8,128)}, f32[8,32,64,64]{3,2,1,0:T(8,128)}, /*...) while((s32[]{:T(128)}, f32[32,64,64]{2,1,0:T(8,128)S(1)}, ...), condition=%wide.region_4.5_spmd.clone, body=%wide.region_3.4_spmd.clone.sunk | while | flops 379937856 | bytes 8534613 | solution.py:102
  57.7 4.3 bitcast_dynamic-update-slice_fusion.7
  68.6 4.3 bitcast_dynamic-update-slice_fusion.7
  74.3 1.8 convolution_add_fusion.2
  79.4 4.3 bitcast_dynamic-update-slice_fusion.7
  90.2 4.3 bitcast_dynamic-update-slice_fusion.7
  101.0 4.3 bitcast_dynamic-update-slice_fusion.7
  111.8 4.2 bitcast_dynamic-update-slice_fusion.7
  122.6 4.2 bitcast_dynamic-update-slice_fusion.7
  133.4 4.3 bitcast_dynamic-update-slice_fusion.7
  143.6 15.3 %all-reduce = f32[256]{0:T(256)S(1)} all-reduce(f32[256]{0:T(256)S(1)} %dynamic-update-slice), channel_id=2, replica_groups=mesh['sec'=4,'dev'=8] {'dev'}, use_global_device_ids=true, to_apply=%add | all-reduce | flops 256 | bytes 2048
  159.0 40.4 %all-gather.8.cloned.1.call-done = f32[256,64,64]{2,1,0:T(8,128)} async-done(((f32[32,64,64]{2,1,0:T(8,128)}), f32[256,64,64]{2,1,0:T(8,128)}) %all-gather.8.cloned.1.call-update) | async-done | bytes 4194320 | tf_op jit(solution)/shard_map/all_gather | solution.py:11
  201.9 66.2 %all-reduce.4.cloned.1.call-done = f32[1,32,64,64]{3,2,1,0:T(8,128)} async-done(((f32[1,32,64,64]{3,2,1,0:T(8,128)}), f32[1,32,64,64]{3,2,1,0:T(8,128)}) %all-reduce.4.cloned.1.call-update) | async-done | bytes 524304 | tf_op jit(solution)/shard_map/psum | solution.py:24
  270.0 11.8 %psum.14 = f32[1,32]{1,0:T(1,128)S(1)} all-reduce(f32[1,32]{1,0:T(1,128)S(1)} %fusion.42), channel_id=1, replica_groups=mesh['sec'=4,'dev'=8] {'dev'}, use_global_device_ids=true, to_apply=%region_7.8 | all-reduce | flops 32 | bytes 256 | tf_op jit(solution)/shard_map/psum | solution.py:24
  281.8 10.8 %all-gather.2 = f32[4,1,32]{2,1,0:T(1,128)S(1)} all-gather(f32[1,1,32]{2,1,0:T(1,128)S(1)} %bitcast.143), channel_id=1, replica_groups=mesh['sec'=4,'dev'=8] {'sec'}, dimensions={0}, use_global_device_ids=true | all-gather | bytes 640 | tf_op jit(solution)/shard_map/all_gather | solution.py:11
  292.6 57.0 %all-gather.6.cloned.1.call-done = f32[4,32,64,64]{3,2,1,0:T(8,128)} async-done(((f32[1,32,64,64]{3,2,1,0:T(8,128)}), f32[4,32,64,64]{3,2,1,0:T(8,128)}) %all-gather.6.cloned.1.call-update) | async-done | bytes 2097168 | tf_op jit(solution)/shard_map/all_gather | solution.py:11
  350.4 16.3 %fusion.37 = bf16[8,256,32,64]{1,3,2,0:T(8,128)(2,1)} fusion(f32[8,256,32,64]{1,3,2,0:T(8,128)} %get-tuple-element.162, bf16[8,256,32,64]{1,3,2,0:T(8,128)(2,1)} %get-tuple-element.592, bf16[8,256,64,1]{2,1,3,0:T(8,128)(2,1)} %bitcast.133, f32[32]{0:T(128)S(1)} %copy-done.8, f32[8,256,32]{1,2,0:T(8,128)S(1)} %get-tuple-element.170, ...), kind=kOutput, calls=%fused_computation.54 | convolution fusion | flops 565182464 | bytes 38798464 | tf_op jit(solution)/shard_map/ktn,khpn->kthp/dot_general | solution.py:123
  366.6 15.4 %copy.39 = bf16[8,256,32,64]{1,0,3,2:T(8,128)(2,1)} copy(bf16[8,256,32,64]{1,3,2,0:T(8,128)(2,1)} %fusion.37) | data formatting | bytes 16777216 | tf_op jit(solution)/shard_map/convert_element_type | solution.py:127
  382.0 10.5 %copy.47 = bf16[256,8,8,256]{3,1,2,0:T(8,128)(2,1)} copy(bf16[256,8,8,256]{3,2,1,0:T(8,128)(2,1)} %bitcast.130) | data formatting | bytes 16777216
  392.5 12.2 %copy.40 = bf16[2048,2048]{1,0:T(8,128)(2,1)} copy(bf16[2048,2048]{0,1:T(8,128)(2,1)} %bitcast.128) | data formatting | bytes 16777216
  404.7 4.6 convolution_bitcast_fusion
  410.8 41.3 %all-reduce.1 = f32[512]{0:T(512)S(1)} all-reduce(f32[512]{0:T(512)S(1)} %bitcast.142), channel_id=4, replica_groups=mesh['sec'=4,'dev'=8] {'sec','dev'}, use_global_device_ids=true, to_apply=%region_14.15.clone | all-reduce | flops 512 | bytes 4096
  (176 shorter events, 62.3 us)
Async XLA Ops:
  7.2 192.2 %all-gather.8.cloned.1.call-start = ((), (), s32[]{:S(2)}) async-start(), calls=%async_computation.2 | async-start | bytes 9437184 | tf_op jit(solution)/shard_map/all_gather | solution.py:11
  33.4 19.5 %copy-start.3 = (bf16[2048,64]{0,1:T(8,128)(2,1)S(1)}, bf16[2048,64]{0,1:T(8,128)(2,1)}, u32[]{:S(2)}) copy-start(bf16[2048,64]{0,1:T(8,128)(2,1)} %param.18) | copy-start | bytes 786436
  33.4 19.7 %copy-start.4 = (f32[2048,32]{0,1:T(8,128)S(1)}, f32[2048,32]{0,1:T(8,128)}, u32[]{:S(2)}) copy-start(f32[2048,32]{0,1:T(8,128)} %param.16) | copy-start | bytes 786436
  54.5 87.7 %copy-start.9 = (u32[32]{0:T(128)S(1)}, u32[32]{0:T(128)}, u32[]{:S(2)}) copy-start(u32[32]{0:T(128)} %constant.91) | copy-start | bytes 388
  141.0 1.1 copy-start
  141.1 58.4 %copy-start.2 = (bf16[8,256,64]{2,1,0:T(8,128)(2,1)}, bf16[8,256,64]{2,1,0:T(8,128)(2,1)S(1)}, u32[]{:S(2)}) copy-start(bf16[8,256,64]{2,1,0:T(8,128)(2,1)S(1)} %get-tuple-element.596) | copy-start | bytes 786436
  142.1 126.0 %all-reduce.4.cloned.1.call-start = ((), (), s32[]{:S(2)}) async-start(), calls=%async_computation | async-start | bytes 2097152 | tf_op jit(solution)/shard_map/psum | solution.py:24
  199.4 1.2 copy-start.1
  199.5 68.6 %copy-start.7 = (bf16[2048]{0:T(1024)(128)(2,1)S(1)}, bf16[2048]{0:T(1024)(128)(2,1)}, u32[]{:S(2)}) copy-start(bf16[2048]{0:T(1024)(128)(2,1)} %param.20) | copy-start | bytes 12292
  199.6 68.6 %copy-start.5 = (s32[512]{0:T(512)S(1)}, s32[512]{0:T(512)}, u32[]{:S(2)}) copy-start(s32[512]{0:T(512)} %param.22) | copy-start | bytes 6148
  199.6 69.2 %copy-start.6 = (s32[512]{0:T(512)S(1)}, s32[512]{0:T(512)}, u32[]{:S(2)}) copy-start(s32[512]{0:T(512)} %param.23) | copy-start | bytes 6148
  201.8 147.8 %all-gather.6.cloned.1.call-start = ((), (), s32[]{:S(2)}) async-start(), calls=%async_computation.1 | async-start | bytes 5242880 | tf_op jit(solution)/shard_map/all_gather | solution.py:11
  349.7 0.7 copy-start.8
Sparse Core Ops, SparseCore 0:
  142.3 57.1 all-gather.7
  202.6 65.5 all-reduce.3
  269.7 79.8 all-gather.5
where the time goes:
time: 462 us; the launch traced here: 459 us
  waiting for transfers between devices  164 us (35%)
  local copies, waits for them, and re-layouts  101 us (22%)
  blocking collectives  79.2 us (17%)
  matrix products  75 us (16%)
  other arithmetic  25.2 us (5%)
  between operations  14.6 us (3%)
    all_gather x2, waiting for transfers between devices, entering(): gathered = jax.tree.map(lambda a: lax.all_gather(a, axis), part)  97.4 us
    psum x1, waiting for transfers between devices, from_root(): return lax.psum(jnp.where(mine, value, jnp.zeros_like(value)), axis)  66.2 us
    unnamed x2, blocking collectives  56.6 us
    unnamed x29, local copies, waits for them, and re-layouts  46.2 us
    dot_general x8, matrix products, local_block(): jnp.einsum('hts,shp->thp', weight, x_heads, preferred_element_type=jnp.fl...  34.1 us
    reshape x1, local copies, waits for them, and re-layouts, shards(): x_blocks = x_input.reshape(count, GROUP, heads, head_size)  24.4 us
    dot_general x1, matrix products, shards(): jnp.einsum('ktn,khpn->kthp', c_blocks, full_state, preferred_element_type...  16.3 us
    convert_element_type x1, local copies, waits for them, and re-layouts, shards(): y_output = mixed.astype(jnp.bfloat16).reshape(rows, width)  15.4 us
  transfers between devices with their start and end apart: 3, of which 3 were waited for; matrix products, arithmetic and copies ran while one was open for 1% of the time, Pallas kernels for 0%

commit v1 on v0

v1 whole, which is shorter than its diff:
```python
import functools
import math

import jax
import jax.numpy as jnp
from jax import lax
from jax.experimental import pallas as pl
from jax.experimental.pallas import tpu as pltpu
from jax.sharding import PartitionSpec as P

CHUNK = 128
LANES = 128
LOG2E = 1.0 / math.log(2.0)
F32 = jnp.float32
BF16 = jnp.bfloat16
VMEM_BYTES = 48 * 1024 * 1024


def iota(shape, dim):
    return lax.broadcasted_iota(jnp.int32, shape, dim)


def my_index():
    return lax.axis_index("sec") * lax.axis_size("dev") + lax.axis_index("dev")


def trace_at(lengths_ref, positions):
    start = jnp.int32(0)
    found = jnp.zeros(jnp.shape(positions), jnp.int32)
    for i in range(lengths_ref.shape[0]):
        found = found + jnp.where(positions >= start, 1, 0)
        start = start + lengths_ref[i]
    return found


def running(decay):
    ones = jnp.where(iota((CHUNK, CHUNK), 0) >= iota((CHUNK, CHUNK), 1), 1.0, 0.0).astype(F32)
    cum = jnp.dot(ones, decay, precision=lax.Precision.HIGHEST, preferred_element_type=F32)
    return cum * LOG2E


def halves(value):
    high = value.astype(BF16)
    low = (value - high.astype(F32)).astype(BF16)
    return jnp.concatenate([high, low], axis=1)


def spread_matrix(heads, width):
    size = width // heads
    row = iota((2 * heads, width), 0)
    head = jnp.where(row >= heads, row - heads, row)
    column = iota((2 * heads, width), 1)
    inside = (column >= head * size) & (column < (head + 1) * size)
    return jnp.where(inside, 1.0, 0.0).astype(BF16)


def state_kernel(count, groups, lengths, x_ref, decay_ref, b_ref, enter_ref, before_ref, send_ref,
                 spread, state, factor):
    k = pl.program_id(0)
    heads, width = decay_ref.shape[1], x_ref.shape[1]

    @pl.when(k == 0)
    def _():
        spread[...] = spread_matrix(heads, width)
        state[...] = jnp.zeros_like(state)
        factor[...] = jnp.ones_like(factor)

    first = (my_index() * count + k) * CHUNK
    cum = running(decay_ref[...])
    trace = trace_at(lengths, first + iota((CHUNK, 1), 0))
    last_trace = trace_at(lengths, jnp.full((1, 1), first + CHUNK - 1, jnp.int32))
    prev_trace = trace_at(lengths, jnp.full((1, 1), first - 1, jnp.int32))
    end = cum[CHUNK - 1:, :]
    to_end = jnp.exp2(end - cum) * jnp.where(trace == last_trace, 1.0, 0.0)
    through = jnp.exp2(end) * jnp.where(last_trace == prev_trace, 1.0, 0.0)
    small = jnp.concatenate([to_end, jnp.broadcast_to(through, (16, heads))], axis=0)
    wide = jnp.dot(halves(small), spread[...], preferred_element_type=F32)
    scaled = (x_ref[...].astype(F32) * wide[:CHUNK]).astype(BF16)
    new = lax.dot_general(b_ref[...], scaled, (((0,), (0,)), ((), ())), preferred_element_type=F32)
    pass_on = wide[CHUNK:CHUNK + 8]
    enter_ref[0] = state[...].astype(BF16)
    before_ref[0] = factor[...]
    state[...] = state[...] * pass_on[:1] + new
    factor[...] = factor[...] * pass_on

    @pl.when(k == count - 1)
    def _():
        rows = state.shape[0] // groups
        for pair in range(width // LANES):
            columns = slice(pair * LANES, (pair + 1) * LANES)
            for g in range(groups):
                send_ref[pair * groups + g, :rows, :] = state[g * rows:(g + 1) * rows, columns]
                send_ref[pair * groups + g, rows:, :] = factor[:, columns]


def greet_all(devices, coords):
    me = my_index()
    barrier = pltpu.get_barrier_semaphore()

    def greet(off, _):
        pl.semaphore_signal(barrier, inc=1, device_id=coords(lax.rem(me + off, devices)),
                            device_id_type=pl.DeviceIdType.MESH)
        return 0

    lax.fori_loop(1, devices, greet, 0)
    pl.semaphore_wait(barrier, devices - 1)


def coordinates(device):
    across = lax.axis_size("dev")
    return (lax.div(device, across), lax.rem(device, across))


def exchange_kernel(devices, groups, send_ref, out_ref, arrived, answers, returned,
                    send_a, recv_a, send_b, recv_b):
    me = my_index()
    rows = answers.shape[1]
    greet_all(devices, coordinates)

    def there(off):
        device = lax.rem(me + off, devices)
        return pltpu.make_async_remote_copy(
            src_ref=send_ref.at[device], dst_ref=arrived.at[me],
            send_sem=send_a.at[off], recv_sem=recv_a.at[off],
            device_id=coordinates(device), device_id_type=pl.DeviceIdType.MESH)

    def back(off):
        device = lax.rem(me + off, devices)
        return pltpu.make_async_remote_copy(
            src_ref=answers.at[device], dst_ref=returned.at[me],
            send_sem=send_b.at[off], recv_sem=recv_b.at[off],
            device_id=coordinates(device), device_id_type=pl.DeviceIdType.MESH)

    def begin(copy):
        def one(off, _):
            copy(off).start()
            return 0
        lax.fori_loop(1, devices, one, 0)

    def finish(copy):
        def one(off, _):
            copy(off).wait()
            return 0
        lax.fori_loop(1, devices, one, 0)

    begin(there)
    arrived[me] = send_ref[me]
    finish(there)

    def step(i, held):
        answers[i] = held
        part = arrived[i]
        return held * part[rows:rows + 1] + part[:rows]

    lax.fori_loop(0, devices, step, jnp.zeros(answers.shape[1:], F32))
    begin(back)
    returned[me] = answers[me]
    finish(back)
    for pair in range(devices // groups):
        for g in range(groups):
            out_ref[g * rows:(g + 1) * rows, pair * LANES:(pair + 1) * LANES] = returned[
                pair * groups + g]


def output_kernel(count, lengths, x_ref, decay_ref, b_ref, c_ref, incoming_ref, enter_ref,
                  before_ref, gain_ref, score_ref, steps_ref, y_ref, part_ref,
                  spread, gain, starts):
    k = pl.program_id(0)
    heads, width = decay_ref.shape[1], x_ref.shape[1]
    lines = steps_ref.shape[0]

    @pl.when(k == 0)
    def _():
        spread[...] = spread_matrix(heads, width)
        gain[...] = jnp.dot(halves(jnp.broadcast_to(gain_ref[...], (16, heads))), spread[...],
                            preferred_element_type=F32)[:8]
        sizes = steps_ref[...].astype(F32)
        upper = jnp.where(iota((LANES, LANES), 0) < iota((LANES, LANES), 1), 1.0, 0.0).astype(F32)
        inner = jnp.dot(sizes, upper, precision=lax.Precision.HIGHEST, preferred_element_type=F32)
        total = jnp.sum(sizes, axis=1, keepdims=True)
        offset = jnp.zeros((1, 1), F32)
        for i in range(lines):
            starts[i:i + 1, :] = inner[i:i + 1, :] + offset
            offset = offset + total[i:i + 1, :]
        part_ref[...] = jnp.zeros_like(part_ref)

    first = (my_index() * count + k) * CHUNK
    cum = running(decay_ref[...])
    cum_rows = cum.T
    trace = trace_at(lengths, first + iota((CHUNK, 1), 0))
    trace_row = trace_at(lengths, first + iota((1, CHUNK), 1))
    prev_trace = trace_at(lengths, jnp.full((1, 1), first - 1, jnp.int32))
    keep = (iota((CHUNK, CHUNK), 0) >= iota((CHUNK, CHUNK), 1)) & (trace == trace_row)
    gram = lax.dot_general(c_ref[...], b_ref[...], (((1,), (1,)), ((), ())),
                           preferred_element_type=F32)
    gram = jnp.where(keep, gram, 0.0)
    carry = halves(jnp.exp2(cum) * jnp.where(trace == prev_trace, 1.0, 0.0))
    low_half = iota((CHUNK, LANES), 1) < LANES // 2
    quad = 2 * LANES
    scores = jnp.zeros((CHUNK, quad), F32)
    per_pair = LANES * heads // width

    def weight(h):
        diff = jnp.minimum(cum[:, h:h + 1] - cum_rows[h:h + 1, :], 0.0)
        return (gram * jnp.exp2(diff)).astype(BF16)

    for q in range(width // quad):
        columns = slice(q * quad, (q + 1) * quad)
        full = (before_ref[0, :1, columns] * incoming_ref[:, columns]
                + enter_ref[0, :, columns].astype(F32)).astype(BF16)
        inter = jnp.dot(c_ref[...], full, preferred_element_type=F32)
        wide = jnp.dot(carry, spread[:, columns], preferred_element_type=F32)
        pieces = []
        for pair in range(2 * q, 2 * q + 2):
            x_pair = x_ref[:, pair * LANES:(pair + 1) * LANES]
            zero = jnp.zeros_like(x_pair)
            both = jnp.concatenate(
                [jnp.where(low_half, x_pair, zero), jnp.where(low_half, zero, x_pair)], axis=0)
            weights = jnp.concatenate([weight(per_pair * pair), weight(per_pair * pair + 1)], axis=1)
            pieces.append(jnp.dot(weights, both, preferred_element_type=F32))
        intra = jnp.concatenate(pieces, axis=1)
        y = (intra + wide * inter + gain[:1, columns] * x_ref[:, columns].astype(F32)).astype(BF16)
        y_ref[:, columns] = y
        scores = scores + y.astype(F32) * score_ref[:1, columns].astype(F32)

    score = jnp.sum(scores, axis=1, keepdims=True)
    places = (first + iota((CHUNK, 1), 0)).astype(F32)
    sizes = steps_ref[...].astype(F32)
    for i in range(lines):
        start = starts[i:i + 1, :]
        inside = (start <= places) & (places < start + sizes[i:i + 1, :])
        part_ref[i:i + 1, :] += jnp.sum(jnp.where(inside, score, 0.0), axis=0, keepdims=True)


def pool_kernel(devices, owned, part_ref, steps_ref, slot_ref, out_ref, arrived, send, recv):
    me = my_index()
    lines = steps_ref.shape[0]
    greet_all(devices, coordinates)

    def copy(off):
        device = lax.rem(me + off, devices)
        return pltpu.make_async_remote_copy(
            src_ref=part_ref, dst_ref=arrived.at[me],
            send_sem=send.at[off], recv_sem=recv.at[off],
            device_id=coordinates(device), device_id_type=pl.DeviceIdType.MESH)

    def begin(off, _):
        copy(off).start()
        return 0

    def finish(off, _):
        copy(off).wait()
        return 0

    lax.fori_loop(1, devices, begin, 0)
    arrived[me] = part_ref[...]
    lax.fori_loop(1, devices, finish, 0)
    total = lax.fori_loop(0, devices, lambda i, t: t + arrived[i], jnp.zeros(part_ref.shape, F32))
    mean = total[:lines] / steps_ref[...].astype(F32)
    slots = me * owned + iota((owned, LANES), 0)
    found = jnp.zeros((owned, LANES), F32)
    for i in range(lines):
        found = found + jnp.where(slot_ref[i:i + 1, :] == slots, mean[i:i + 1, :], 0.0)
    out_ref[...] = jnp.broadcast_to(jnp.sum(found, axis=1, keepdims=True), (owned, LANES))


def shards(x_input, log_decay, b_input, c_input, skip_gain, score_weight, trace_lengths,
           step_lengths, step_slot):
    rows, width = x_input.shape
    heads = log_decay.shape[1]
    state_size = b_input.shape[1]
    count = rows // CHUNK
    devices = lax.axis_size(("sec", "dev"))
    groups = devices // (width // LANES)
    depth = state_size // groups
    steps = step_slot.shape[0]
    lines = steps // LANES
    owned = steps // devices
    whole = pl.BlockSpec(memory_space=pltpu.VMEM)
    scalar = pl.BlockSpec(memory_space=pltpu.SMEM)

    def by_chunk(columns):
        return pl.BlockSpec((CHUNK, columns), lambda k: (k, 0))

    def by_chunk3(a, b):
        return pl.BlockSpec((1, a, b), lambda k: (k, 0, 0))

    def fixed(*shape):
        return pl.BlockSpec(shape, lambda k: (0,) * len(shape))

    enter, before, send = pl.pallas_call(
        functools.partial(state_kernel, count, groups),
        grid=(count,),
        in_specs=[scalar, by_chunk(width), by_chunk(heads), by_chunk(state_size)],
        out_specs=[by_chunk3(state_size, width), by_chunk3(8, width),
                   fixed(devices, depth + 8, LANES)],
        out_shape=[jax.ShapeDtypeStruct((count, state_size, width), BF16),
                   jax.ShapeDtypeStruct((count, 8, width), F32),
                   jax.ShapeDtypeStruct((devices, depth + 8, LANES), F32)],
        scratch_shapes=[pltpu.VMEM((2 * heads, width), BF16), pltpu.VMEM((state_size, width), F32),
                        pltpu.VMEM((8, width), F32)],
        compiler_params=pltpu.CompilerParams(vmem_limit_bytes=VMEM_BYTES),
        name="chunk_states",
    )(trace_lengths, x_input, log_decay, b_input)

    sems = pltpu.SemaphoreType.DMA((devices,))
    incoming = pl.pallas_call(
        functools.partial(exchange_kernel, devices, groups),
        in_specs=[whole],
        out_specs=whole,
        out_shape=jax.ShapeDtypeStruct((state_size, width), F32),
        scratch_shapes=[pltpu.VMEM((devices, depth + 8, LANES), F32),
                        pltpu.VMEM((devices, depth, LANES), F32),
                        pltpu.VMEM((devices, depth, LANES), F32), sems, sems, sems, sems],
        compiler_params=pltpu.CompilerParams(collective_id=0, has_side_effects=True,
                                             vmem_limit_bytes=VMEM_BYTES),
        name="state_exchange",
    )(send)

    lines8 = max(8, lines)
    steps_rows = step_lengths.reshape(lines, LANES)
    y_output, part = pl.pallas_call(
        functools.partial(output_kernel, count),
        grid=(count,),
        in_specs=[scalar, by_chunk(width), by_chunk(heads), by_chunk(state_size),
                  by_chunk(state_size), fixed(state_size, width), by_chunk3(state_size, width),
                  by_chunk3(8, width), fixed(1, heads), fixed(1, width), fixed(lines, LANES)],
        out_specs=[by_chunk(width), fixed(lines8, LANES)],
        out_shape=[jax.ShapeDtypeStruct((rows, width), BF16),
                   jax.ShapeDtypeStruct((lines8, LANES), F32)],
        scratch_shapes=[pltpu.VMEM((2 * heads, width), BF16), pltpu.VMEM((8, width), F32),
                        pltpu.VMEM((lines8, LANES), F32)],
        compiler_params=pltpu.CompilerParams(vmem_limit_bytes=VMEM_BYTES),
        name="outputs",
    )(trace_lengths, x_input, log_decay, b_input, c_input, incoming, enter, before,
      skip_gain.reshape(1, heads), score_weight.reshape(1, width), steps_rows)

    pooled = pl.pallas_call(
        functools.partial(pool_kernel, devices, owned),
        in_specs=[whole, whole, whole],
        out_specs=whole,
        out_shape=jax.ShapeDtypeStruct((owned, LANES), F32),
        scratch_shapes=[pltpu.VMEM((devices, lines8, LANES), F32), sems, sems],
        compiler_params=pltpu.CompilerParams(collective_id=1, has_side_effects=True,
                                             vmem_limit_bytes=VMEM_BYTES),
        name="step_pool",
    )(part, steps_rows, step_slot.reshape(lines, LANES))
    return (y_output, pooled[:, 0])


def solution(mesh):
    tokens = P(("sec", "dev"), None)
    return jax.shard_map(
        shards,
        mesh=mesh,
        in_specs=(tokens, tokens, tokens, tokens, P(), P(), P(), P(), P()),
        out_specs=(tokens, P(("sec", "dev"))),
        check_vma=False,
    )
```

time: 462 us -> 95.7 us (0.21)
  waiting for transfers between devices: 164 us -> 0 us
  local copies, waits for them, and re-layouts: 101 us -> 5.73 us
  Pallas kernels: 0 us -> 88.6 us
  blocking collectives: 79.2 us -> 0 us
  matrix products: 75 us -> 0 us
  other arithmetic: 25.2 us -> 0 us
  between operations: 14.6 us -> 0.72 us
    all_gather x2 -> x0, waiting for transfers between devices: 97.4 us -> none  [entering(): gathered = jax.tree.map(lambda a: lax.all_gather(a, axis), part)]
    pallas_call x0 -> x4, Pallas kernels: none -> 88.6 us  [the longest x1 32.7 us: shards(): pl.pallas_call(functools.partial(exchange_kernel, devices, groups), in_sp...]
    dot_general x35 -> x0, matrix products: 75 us -> none  [the longest x8 34.1 us: local_block(): jnp.einsum('hts,shp->thp', weight, x_heads, preferred_element_type=jnp.fl...]
    psum x1 -> x0, waiting for transfers between devices: 66.2 us -> none  [from_root(): return lax.psum(jnp.where(mine, value, jnp.zeros_like(value)), axis)]
    unnamed x2 -> x0, blocking collectives: 56.6 us -> none
    unnamed x29 -> x11, local copies, waits for them, and re-layouts: 46.2 us -> 4.4 us
    reshape x3 -> x1, local copies, waits for them, and re-layouts: 25.4 us -> 0.71 us  [shards(): score_weight.reshape(1, width)]
    convert_element_type x1 -> x0, local copies, waits for them, and re-layouts: 15.4 us -> none  [shards(): y_output = mixed.astype(jnp.bfloat16).reshape(rows, width)]
  transfers between devices with their start and end apart: 3 -> 0, of which waited for: 3 -> 0; matrix products, arithmetic and copies ran while one was open for 1% -> 0% of each run, Pallas kernels for 0% -> 0%
where the time goes in v1:
time: 95.7 us; the launch traced here: 95.1 us
  Pallas kernels  88.6 us (93%)
  local copies, waits for them, and re-layouts  5.73 us (6%)
    pallas_call x1, Pallas kernels, shards(): pl.pallas_call(functools.partial(exchange_kernel, devices, groups), in_sp...  32.7 us
    pallas_call x1, Pallas kernels, shards(): pl.pallas_call(functools.partial(output_kernel, count), grid=(count,), in...  26.2 us
    pallas_call x1, Pallas kernels, shards(): pl.pallas_call(functools.partial(state_kernel, count, groups), grid=(coun...  17.3 us
    pallas_call x1, Pallas kernels, shards(): pl.pallas_call(functools.partial(pool_kernel, devices, owned), in_specs=[...  12.5 us
    unnamed x11, local copies, waits for them, and re-layouts  4.4 us

profile of v1, /device:TPU:0, one launch (start us, length us, event | category | flops | bytes accessed | tf_op | source)
XLA Modules:
  0.0 95.1 jit_solution(10946559074974238052)
XLA Ops:
  0.6 0.0 copy-start
  0.6 0.0 copy-start.3
  0.7 0.7 reshape.17.score_ref
  1.4 1.2 %copy.19.b_ref = bf16[2048,64]{1,0:T(8,128)(2,1)S(1)} copy(bf16[2048,64]{0,1:T(8,128)(2,1)} %param.11) | data formatting | bytes 524288 | tf_op args[2]
  2.6 1.2 %copy.20.c_ref = bf16[2048,64]{1,0:T(8,128)(2,1)S(1)} copy(bf16[2048,64]{0,1:T(8,128)(2,1)} %param.12) | data formatting | bytes 524288 | tf_op args[3]
  3.8 1.3 %copy.18.decay_ref = f32[2048,32]{1,0:T(8,128)S(1)} copy(f32[2048,32]{0,1:T(8,128)} %param.10) | data formatting | bytes 524288 | tf_op args[1]
  5.1 0.0 copy-start.1
  5.1 0.6 copy-done.1
  5.8 17.3 %chunk_states.1 = (bf16[16,64,2048]{2,1,0:T(8,128)(2,1)}, f32[16,8,2048]{2,1,0:T(8,128)S(1)}, f32[32,40,128]{2,1,0:T(8,128)S(1)}) custom-call(s32[4]{0:T(128)S(1)} %copy-done.1, bf16[2048,2048]{1,0:T(8,128)(2,1)} %x_ref.3, f32[2048,32]{1,0:T(8,128)S(1)} %copy.18.decay_ref, bf16[2048,64]{1,0:T(8,128)(2,1)S(1)} %copy.19.b_ref), custom_call_target="tpu_custom_call" | custom-call | tf_op jit(solution)/shard_map/chunk_states/pallas_call | solution.py:291
  23.0 32.7 %state_exchange.1.incoming_ref = f32[64,2048]{1,0:T(8,128)S(1)} custom-call(f32[32,40,128]{2,1,0:T(8,128)S(1)} %get-tuple-element.7.send_ref), custom_call_target="tpu_custom_call" | custom-call | tf_op jit(solution)/shard_map/state_exchange/pallas_call | solution.py:307
  55.8 0.0 copy-done
  55.8 0.0 copy-done.3
  55.8 0.0 copy-start.2
  55.8 26.2 %outputs.1 = (bf16[2048,2048]{1,0:T(8,128)(2,1)}, f32[8,128]{1,0:T(8,128)S(1)}) custom-call(s32[4]{0:T(128)S(1)} %copy-done.1, bf16[2048,2048]{1,0:T(8,128)(2,1)} %x_ref.3, f32[2048,32]{1,0:T(8,128)S(1)} %copy.18.decay_ref, bf16[2048,64]{1,0:T(8,128)(2,1)S(1)} %copy.19.b_ref, bf16[2048,64]{1,0:T(8,128)(2,1)S(1)} %copy.20.c_ref, ...), custom_call_target="tpu_custom_call" | custom-call | tf_op jit(solution)/shard_map/outputs/pallas_call | solution.py:322
  82.0 0.0 copy-done.2
  82.0 12.5 %step_pool.1 = f32[16,128]{1,0:T(8,128)S(1)} custom-call(f32[8,128]{1,0:T(8,128)S(1)} %get-tuple-element.11.part_ref, s32[4,128]{1,0:T(4,128)S(1)} %bitcast.4, s32[4,128]{1,0:T(4,128)S(1)} %bitcast.5), custom_call_target="tpu_custom_call" | custom-call | tf_op jit(solution)/shard_map/step_pool/pallas_call | solution.py:338
  94.4 0.6 slice_reduce_fusion
Async XLA Ops:
  0.6 55.1 %copy-start = (s32[512]{0:T(512)S(1)}, s32[512]{0:T(512)}, u32[]{:S(2)}) copy-start(s32[512]{0:T(512)} %param.16) | copy-start | bytes 6148
  0.6 55.1 %copy-start.3 = (f32[32]{0:T(128)S(1)}, f32[32]{0:T(128)}, u32[]{:S(2)}) copy-start(f32[32]{0:T(128)} %param.13) | copy-start | bytes 388
  5.1 0.7 copy-start.1
  55.8 26.2 %copy-start.2 = (s32[512]{0:T(512)S(1)}, s32[512]{0:T(512)}, u32[]{:S(2)}) copy-start(s32[512]{0:T(512)} %param.17) | copy-start | bytes 6148

commit v2 on v1

v2 whole, which is shorter than its diff:
```python
import functools
import math

import jax
import jax.numpy as jnp
from jax import lax
from jax.experimental import pallas as pl
from jax.experimental.pallas import tpu as pltpu
from jax.sharding import PartitionSpec as P

CHUNK = 128
STATE_CHUNKS = 4
OUTPUT_CHUNKS = 2
LANES = 128
LOG2E = 1.0 / math.log(2.0)
F32 = jnp.float32
BF16 = jnp.bfloat16
VMEM_BYTES = 60 * 1024 * 1024


def iota(shape, dim):
    return lax.broadcasted_iota(jnp.int32, shape, dim)


def my_index():
    return lax.axis_index("sec") * lax.axis_size("dev") + lax.axis_index("dev")


def trace_at(lengths_ref, positions):
    start = jnp.int32(0)
    found = jnp.zeros(jnp.shape(positions), jnp.int32)
    for i in range(lengths_ref.shape[0]):
        found = found + jnp.where(positions >= start, 1, 0)
        start = start + lengths_ref[i]
    return found


def running(decay_rows):
    ones = jnp.where(iota((CHUNK, CHUNK), 0) <= iota((CHUNK, CHUNK), 1), 1.0, 0.0).astype(F32)
    cum = jnp.dot(decay_rows, ones, precision=lax.Precision.HIGHEST, preferred_element_type=F32)
    return cum * LOG2E


def halves(value):
    high = value.astype(BF16)
    low = (value - high.astype(F32)).astype(BF16)
    return jnp.concatenate([high, low], axis=1)


def spread_matrix(heads, width):
    size = width // heads
    row = iota((2 * heads, width), 0)
    head = jnp.where(row >= heads, row - heads, row)
    column = iota((2 * heads, width), 1)
    inside = (column >= head * size) & (column < (head + 1) * size)
    return jnp.where(inside, 1.0, 0.0).astype(BF16)


def state_kernel(count, groups, lengths, x_ref, decay_ref, b_ref, enter_ref, before_ref, send_ref,
                 spread, state, factor):
    k = pl.program_id(0)
    heads, width = decay_ref.shape[0], x_ref.shape[1]

    @pl.when(k == 0)
    def _():
        spread[...] = spread_matrix(heads, width)
        state[...] = jnp.zeros_like(state)
        factor[...] = jnp.ones_like(factor)

    ends, passes = [], jnp.zeros((heads, LANES), F32)
    for sub in range(STATE_CHUNKS):
        tokens = slice(sub * CHUNK, (sub + 1) * CHUNK)
        first = (my_index() * count + k * STATE_CHUNKS + sub) * CHUNK
        cum = running(decay_ref[:, tokens])
        trace = trace_at(lengths, first + iota((1, CHUNK), 1))
        last_trace = trace_at(lengths, jnp.full((1, 1), first + CHUNK - 1, jnp.int32))
        prev_trace = trace_at(lengths, jnp.full((1, 1), first - 1, jnp.int32))
        end = cum[:, CHUNK - 1:]
        ends.append(jnp.exp2(end - cum) * jnp.where(trace == last_trace, 1.0, 0.0))
        through = jnp.exp2(end) * jnp.where(last_trace == prev_trace, 1.0, 0.0)
        passes = passes + jnp.where(iota((heads, LANES), 1) == sub, through, 0.0)
    pass_on = jnp.dot(halves(passes.T[:16]), spread[...], preferred_element_type=F32)

    inputs = [b_ref[:, sub * CHUNK:(sub + 1) * CHUNK].astype(F32) for sub in range(STATE_CHUNKS)]
    states = state.shape[0]
    low_half = iota((states, LANES), 1) < LANES // 2
    for pair in range(width // LANES):
        columns = slice(pair * LANES, (pair + 1) * LANES)
        held, product = state[:, columns], factor[:, columns]
        for sub in range(STATE_CHUNKS):
            tokens = slice(sub * CHUNK, (sub + 1) * CHUNK)
            both = jnp.concatenate(
                [(inputs[sub] * ends[sub][h:h + 1, :]).astype(BF16) for h in (2 * pair, 2 * pair + 1)],
                axis=0)
            new = jnp.dot(both, x_ref[tokens, columns], preferred_element_type=F32)
            step = pass_on[sub:sub + 1, columns]
            enter_ref[sub, :, columns] = held.astype(BF16)
            before_ref[sub, :, columns] = product
            held = held * step + jnp.where(low_half, new[:states], new[states:])
            product = product * step
        state[:, columns] = held
        factor[:, columns] = product

    @pl.when(k == count // STATE_CHUNKS - 1)
    def _():
        rows = state.shape[0] // groups
        for pair in range(width // LANES):
            columns = slice(pair * LANES, (pair + 1) * LANES)
            for g in range(groups):
                send_ref[pair * groups + g, :rows, :] = state[g * rows:(g + 1) * rows, columns]
                send_ref[pair * groups + g, rows:, :] = factor[:, columns]


def wrapped(index, size):
    return index - jnp.where(index >= size, size, 0)


def each(low, high, action):
    def one(i, _):
        action(i)
        return 0

    lax.fori_loop(low, high, one, 0)


def greet(coords):
    pl.semaphore_signal(pltpu.get_barrier_semaphore(), inc=1, device_id=coords,
                        device_id_type=pl.DeviceIdType.MESH)


def exchange_kernel(chips, groups, send_ref, out_ref, other, chip, arrived, answers, returned,
                    theirs, last, pair_send, pair_recv, send_a, recv_a, send_b, recv_b):
    sec, dev = lax.axis_index("sec"), lax.axis_index("dev")
    per_sec = lax.axis_size("dev") // 2
    core = lax.rem(dev, 2)
    here = sec * per_sec + lax.div(dev, 2)
    early = core == 0
    partner = (sec, dev + 1 - 2 * core)
    rows = answers.shape[1]

    def peer(off):
        place = wrapped(here + off, chips)
        return place, (lax.div(place, per_sec), lax.rem(place, per_sec) * 2 + core)

    each(1, chips, lambda off: greet(peer(off)[1]))
    greet(partner)
    pl.semaphore_wait(pltpu.get_barrier_semaphore(), chips)

    def to_partner(n, source, target):
        return pltpu.make_async_remote_copy(
            src_ref=source, dst_ref=target, send_sem=pair_send.at[n], recv_sem=pair_recv.at[n],
            device_id=partner, device_id_type=pl.DeviceIdType.MESH)

    def to_peer(off, source, target, send, recv):
        place, coords = peer(off)
        return pltpu.make_async_remote_copy(
            src_ref=source.at[place], dst_ref=target.at[here], send_sem=send.at[off],
            recv_sem=recv.at[off], device_id=coords, device_id_type=pl.DeviceIdType.MESH)

    def there(off):
        return to_peer(off, chip, arrived, send_a, recv_a)

    def back(off):
        return to_peer(off, answers, returned, send_b, recv_b)

    def combine(p):
        own, his = send_ref[core * chips + p], other[p]
        before, after = jnp.where(early, own, his), jnp.where(early, his, own)
        pass_on = after[rows:rows + 1]
        return before[:rows] * pass_on + after[:rows], before[rows:] * after[rows:]

    first = to_partner(0, send_ref.at[pl.ds((1 - core) * chips, chips)], other)
    first.start()
    first.wait()

    def put(off):
        place, _ = peer(off)
        total, product = combine(place)
        chip[place, :rows] = total
        chip[place, rows:] = product
        there(off).start()

    each(1, chips, put)
    total, product = combine(here)
    arrived[here, :rows] = total
    arrived[here, rows:] = product
    each(1, chips, lambda off: there(off).wait())

    def step(i, held):
        answers[i] = held
        part = arrived[i]
        return held * part[rows:rows + 1] + part[:rows]

    lax.fori_loop(0, chips, step, jnp.zeros(answers.shape[1:], F32))
    each(1, chips, lambda off: back(off).start())
    returned[here] = answers[here]
    each(1, chips, lambda off: back(off).wait())

    def split(p):
        part = jnp.where(early, send_ref[core * chips + p], other[p])
        enters = returned[p]
        leaves = enters * part[rows:rows + 1] + part[:rows]
        theirs[p] = jnp.where(early, leaves, enters)
        returned[p] = jnp.where(early, enters, leaves)

    each(0, chips, split)
    final = to_partner(1, theirs, last)
    final.start()
    final.wait()
    for half in range(2):
        for p in range(chips):
            pair, g = divmod(half * chips + p, groups)
            out_ref[g * rows:(g + 1) * rows, pair * LANES:(pair + 1) * LANES] = jnp.where(
                core == half, returned[p], last[p])


def output_kernel(count, lengths, x_ref, decay_ref, b_ref, c_ref, incoming_ref, enter_ref,
                  before_ref, gain_ref, score_ref, steps_ref, y_ref, part_ref,
                  spread, gain, starts):
    k = pl.program_id(0)
    heads, width = decay_ref.shape[0], x_ref.shape[1]
    lines = steps_ref.shape[0]

    @pl.when(k == 0)
    def _():
        spread[...] = spread_matrix(heads, width)
        gain[...] = jnp.dot(halves(jnp.broadcast_to(gain_ref[...], (16, heads))), spread[...],
                            preferred_element_type=F32)[:8]
        sizes = steps_ref[...].astype(F32)
        upper = jnp.where(iota((LANES, LANES), 0) < iota((LANES, LANES), 1), 1.0, 0.0).astype(F32)
        inner = jnp.dot(sizes, upper, precision=lax.Precision.HIGHEST, preferred_element_type=F32)
        total = jnp.sum(sizes, axis=1, keepdims=True)
        offset = jnp.zeros((1, 1), F32)
        for i in range(lines):
            starts[i:i + 1, :] = inner[i:i + 1, :] + offset
            offset = offset + total[i:i + 1, :]
        part_ref[...] = jnp.zeros_like(part_ref)

    for sub in range(OUTPUT_CHUNKS):
        first = (my_index() * count + k * OUTPUT_CHUNKS + sub) * CHUNK
        tokens = slice(sub * CHUNK, (sub + 1) * CHUNK)
        cum_rows = running(decay_ref[:, tokens])
        cum = cum_rows.T
        c = c_ref[:, tokens].T
        trace = trace_at(lengths, first + iota((CHUNK, 1), 0))
        trace_row = trace_at(lengths, first + iota((1, CHUNK), 1))
        prev_trace = trace_at(lengths, jnp.full((1, 1), first - 1, jnp.int32))
        keep = (iota((CHUNK, CHUNK), 0) >= iota((CHUNK, CHUNK), 1)) & (trace == trace_row)
        gram = jnp.dot(c, b_ref[:, tokens], preferred_element_type=F32)
        gram = jnp.where(keep, gram, 0.0)
        c_kept = jnp.where(trace == prev_trace, c.astype(F32), 0.0).astype(BF16)
        low_half = iota((CHUNK, LANES), 1) < LANES // 2
        quad = 2 * LANES
        scores = jnp.zeros((CHUNK, LANES), F32)

        def weight(h):
            here = jnp.broadcast_to(cum[:, h:h + 1], (CHUNK, CHUNK))
            diff = jnp.minimum(here - cum_rows[h:h + 1, :], 0.0)
            return here, (gram * jnp.exp2(diff)).astype(BF16)

        for q in range(width // quad):
            wide = slice(q * quad, (q + 1) * quad)
            full = (before_ref[sub, :1, wide] * incoming_ref[:, wide]
                    + enter_ref[sub, :, wide].astype(F32)).astype(BF16)
            inter = jnp.dot(c_kept, full, preferred_element_type=F32)
            for half in range(2):
                pair = 2 * q + half
                columns = slice(pair * LANES, (pair + 1) * LANES)
                x_pair = x_ref[tokens, columns]
                zero = jnp.zeros_like(x_pair)
                both = jnp.concatenate(
                    [jnp.where(low_half, x_pair, zero), jnp.where(low_half, zero, x_pair)], axis=0)
                here_a, weight_a = weight(2 * pair)
                here_b, weight_b = weight(2 * pair + 1)
                intra = jnp.dot(jnp.concatenate([weight_a, weight_b], axis=1), both,
                                preferred_element_type=F32)
                carry = jnp.exp2(jnp.where(low_half, here_a, here_b))
                y = (intra + carry * inter[:, half * LANES:(half + 1) * LANES]
                     + gain[:1, columns] * x_pair.astype(F32)).astype(BF16)
                y_ref[tokens, columns] = y
                scores = scores + y.astype(F32) * score_ref[:1, columns].astype(F32)

        score = jnp.sum(scores, axis=1, keepdims=True)
        places = (first + iota((CHUNK, 1), 0)).astype(F32)
        sizes = steps_ref[...].astype(F32)
        for i in range(lines):
            start = starts[i:i + 1, :]
            inside = (start <= places) & (places < start + sizes[i:i + 1, :])
            part_ref[i:i + 1, :] += jnp.sum(jnp.where(inside, score, 0.0), axis=0, keepdims=True)


def pool_kernel(owned, part_ref, steps_ref, slot_ref, out_ref, near, sums, far,
                send_a, recv_a, send_b, recv_b):
    sec, dev = lax.axis_index("sec"), lax.axis_index("dev")
    secs, devs = lax.axis_size("sec"), lax.axis_size("dev")
    lines = steps_ref.shape[0]

    def beside(off):
        return (sec, wrapped(dev + off, devs))

    def across(off):
        return (wrapped(sec + off, secs), dev)

    def inner(off):
        return pltpu.make_async_remote_copy(
            src_ref=part_ref, dst_ref=near.at[dev], send_sem=send_a.at[off],
            recv_sem=recv_a.at[off], device_id=beside(off), device_id_type=pl.DeviceIdType.MESH)

    def outer(off):
        return pltpu.make_async_remote_copy(
            src_ref=sums, dst_ref=far.at[sec], send_sem=send_b.at[off],
            recv_sem=recv_b.at[off], device_id=across(off), device_id_type=pl.DeviceIdType.MESH)

    each(1, devs, lambda off: greet(beside(off)))
    each(1, secs, lambda off: greet(across(off)))
    pl.semaphore_wait(pltpu.get_barrier_semaphore(), devs + secs - 2)
    each(1, devs, lambda off: inner(off).start())
    near[dev] = part_ref[...]
    each(1, devs, lambda off: inner(off).wait())
    sums[...] = jnp.sum(near[...], axis=0)
    each(1, secs, lambda off: outer(off).start())
    far[sec] = sums[...]
    each(1, secs, lambda off: outer(off).wait())
    mean = jnp.sum(far[...], axis=0)[:lines] / steps_ref[...].astype(F32)
    slots = my_index() * owned + iota((owned, LANES), 0)
    found = jnp.zeros((owned, LANES), F32)
    for i in range(lines):
        found = found + jnp.where(slot_ref[i:i + 1, :] == slots, mean[i:i + 1, :], 0.0)
    out_ref[...] = jnp.broadcast_to(jnp.sum(found, axis=1, keepdims=True), (owned, LANES))


def shards(x_input, log_decay, b_input, c_input, skip_gain, score_weight, trace_lengths,
           step_lengths, step_slot):
    rows, width = x_input.shape
    heads = log_decay.shape[1]
    state_size = b_input.shape[1]
    count = rows // CHUNK
    devices = lax.axis_size(("sec", "dev"))
    groups = devices // (width // LANES)
    depth = state_size // groups
    steps = step_slot.shape[0]
    lines = steps // LANES
    owned = steps // devices
    whole = pl.BlockSpec(memory_space=pltpu.VMEM)
    scalar = pl.BlockSpec(memory_space=pltpu.SMEM)

    chips = devices // 2
    sections, across = lax.axis_size("sec"), lax.axis_size("dev")
    decay_rows, b_rows, c_rows = log_decay.T, b_input.T, c_input.T

    def by_chunk(n):
        return pl.BlockSpec((n * CHUNK, width), lambda k: (k, 0))

    def by_row(n, lines):
        return pl.BlockSpec((lines, n * CHUNK), lambda k: (0, k))

    def by_chunk3(n, a, b):
        return pl.BlockSpec((n, a, b), lambda k: (k, 0, 0))

    def fixed(*shape):
        return pl.BlockSpec(shape, lambda k: (0,) * len(shape))

    enter, before, send = pl.pallas_call(
        functools.partial(state_kernel, count, groups),
        grid=(count // STATE_CHUNKS,),
        in_specs=[scalar, by_chunk(STATE_CHUNKS), by_row(STATE_CHUNKS, heads),
                  by_row(STATE_CHUNKS, state_size)],
        out_specs=[by_chunk3(STATE_CHUNKS, state_size, width), by_chunk3(STATE_CHUNKS, 8, width),
                   fixed(devices, depth + 8, LANES)],
        out_shape=[jax.ShapeDtypeStruct((count, state_size, width), BF16),
                   jax.ShapeDtypeStruct((count, 8, width), F32),
                   jax.ShapeDtypeStruct((devices, depth + 8, LANES), F32)],
        scratch_shapes=[pltpu.VMEM((2 * heads, width), BF16), pltpu.VMEM((state_size, width), F32),
                        pltpu.VMEM((8, width), F32)],
        compiler_params=pltpu.CompilerParams(vmem_limit_bytes=VMEM_BYTES),
        name="chunk_states",
    )(trace_lengths, x_input, decay_rows, b_rows)

    def sems(n):
        return pltpu.SemaphoreType.DMA((n,))

    def blocks(lines):
        return pltpu.VMEM((chips, lines, LANES), F32)

    incoming = pl.pallas_call(
        functools.partial(exchange_kernel, chips, groups),
        in_specs=[whole],
        out_specs=whole,
        out_shape=jax.ShapeDtypeStruct((state_size, width), F32),
        scratch_shapes=[blocks(depth + 8), blocks(depth + 8), blocks(depth + 8), blocks(depth),
                        blocks(depth), blocks(depth), blocks(depth), sems(2), sems(2),
                        sems(chips), sems(chips), sems(chips), sems(chips)],
        compiler_params=pltpu.CompilerParams(collective_id=0, has_side_effects=True,
                                             vmem_limit_bytes=VMEM_BYTES),
        name="state_exchange",
    )(send)

    lines8 = max(8, lines)
    steps_rows = step_lengths.reshape(lines, LANES)
    y_output, part = pl.pallas_call(
        functools.partial(output_kernel, count),
        grid=(count // OUTPUT_CHUNKS,),
        in_specs=[scalar, by_chunk(OUTPUT_CHUNKS), by_row(OUTPUT_CHUNKS, heads),
                  by_row(OUTPUT_CHUNKS, state_size), by_row(OUTPUT_CHUNKS, state_size),
                  fixed(state_size, width), by_chunk3(OUTPUT_CHUNKS, state_size, width),
                  by_chunk3(OUTPUT_CHUNKS, 8, width), fixed(1, heads), fixed(1, width), fixed(lines, LANES)],
        out_specs=[by_chunk(OUTPUT_CHUNKS), fixed(lines8, LANES)],
        out_shape=[jax.ShapeDtypeStruct((rows, width), BF16),
                   jax.ShapeDtypeStruct((lines8, LANES), F32)],
        scratch_shapes=[pltpu.VMEM((2 * heads, width), BF16), pltpu.VMEM((8, width), F32),
                        pltpu.VMEM((lines8, LANES), F32)],
        compiler_params=pltpu.CompilerParams(vmem_limit_bytes=VMEM_BYTES),
        name="outputs",
    )(trace_lengths, x_input, decay_rows, b_rows, c_rows, incoming, enter, before,
      skip_gain.reshape(1, heads), score_weight.reshape(1, width), steps_rows)

    pooled = pl.pallas_call(
        functools.partial(pool_kernel, owned),
        in_specs=[whole, whole, whole],
        out_specs=whole,
        out_shape=jax.ShapeDtypeStruct((owned, LANES), F32),
        scratch_shapes=[pltpu.VMEM((across, lines8, LANES), F32), pltpu.VMEM((lines8, LANES), F32),
                        pltpu.VMEM((sections, lines8, LANES), F32), sems(across), sems(across),
                        sems(sections), sems(sections)],
        compiler_params=pltpu.CompilerParams(collective_id=1, has_side_effects=True,
                                             vmem_limit_bytes=VMEM_BYTES),
        name="step_pool",
    )(part, steps_rows, step_slot.reshape(lines, LANES))
    return (y_output, pooled[:, 0])


def solution(mesh):
    tokens = P(("sec", "dev"), None)
    return jax.shard_map(
        shards,
        mesh=mesh,
        in_specs=(tokens, tokens, tokens, tokens, P(), P(), P(), P(), P()),
        out_specs=(tokens, P(("sec", "dev"))),
        check_vma=False,
    )
```

time: 95.7 us -> 79.3 us (0.83)
  Pallas kernels: 88.6 us -> 75.7 us
  local copies, waits for them, and re-layouts: 5.73 us -> 2.61 us
    pallas_call x1, Pallas kernels: 17.3 us -> 10.2 us  [shards(): pl.pallas_call(functools.partial(state_kernel, count, groups), grid=(coun...]
    pallas_call x3, Pallas kernels: 71.3 us -> 65.5 us  [the longest x1 27.4 us: shards(): pl.pallas_call(functools.partial(exchange_kernel, chips, groups), in_spec...]
    unnamed x11 -> x0, local copies, waits for them, and re-layouts: 4.4 us -> none
where the time goes in v2:
time: 79.3 us; the launch traced here: 79 us
  Pallas kernels  75.7 us (95%)
  local copies, waits for them, and re-layouts  2.61 us (3%)
    pallas_call x1, Pallas kernels, shards(): pl.pallas_call(functools.partial(exchange_kernel, chips, groups), in_spec...  27.4 us
    pallas_call x1, Pallas kernels, shards(): pl.pallas_call(functools.partial(output_kernel, count), grid=(count // OU...  26.1 us
    pallas_call x1, Pallas kernels, shards(): pl.pallas_call(functools.partial(pool_kernel, owned), in_specs=[whole, wh...  11.9 us
    pallas_call x1, Pallas kernels, shards(): pl.pallas_call(functools.partial(state_kernel, count, groups), grid=(coun...  10.2 us

profile of v2, /device:TPU:0, one launch (start us, length us, event | category | flops | bytes accessed | tf_op | source)
XLA Modules:
  0.0 79.0 jit_solution(16733369543991422721)
XLA Ops:
  0.6 1.3 %reshape.17.score_ref = bf16[1,2048]{1,0:T(2,128)(2,1)} reshape(bf16[2048]{0:T(1024)(128)(2,1)} %param.14) | data formatting | bytes 8192 | tf_op jit(solution)/shard_map/reshape | solution.py:415
  1.9 10.2 %chunk_states.1 = (bf16[16,64,2048]{2,1,0:T(8,128)(2,1)}, f32[16,8,2048]{2,1,0:T(8,128)}, f32[32,40,128]{2,1,0:T(8,128)}) custom-call(s32[4]{0:T(128)} %lengths.3, bf16[2048,2048]{1,0:T(8,128)(2,1)} %x_ref.3, f32[32,2048]{1,0:T(8,128)} %bitcast.6, bf16[64,2048]{1,0:T(8,128)(2,1)} %bitcast.8), custom_call_target="tpu_custom_call" | custom-call | tf_op jit(solution)/shard_map/chunk_states/pallas_call | solution.py:363
  12.1 27.4 %state_exchange.1.incoming_ref = f32[64,2048]{1,0:T(8,128)} custom-call(f32[32,40,128]{2,1,0:T(8,128)} %get-tuple-element.7.send_ref), custom_call_target="tpu_custom_call" | custom-call | tf_op jit(solution)/shard_map/state_exchange/pallas_call | solution.py:385
  39.6 26.1 %outputs.1 = (bf16[2048,2048]{1,0:T(8,128)(2,1)}, f32[8,128]{1,0:T(8,128)}) custom-call(s32[4]{0:T(128)} %lengths.3, bf16[2048,2048]{1,0:T(8,128)(2,1)} %x_ref.3, f32[32,2048]{1,0:T(8,128)} %bitcast.7, bf16[64,2048]{1,0:T(8,128)(2,1)} %bitcast.9, bf16[64,2048]{1,0:T(8,128)(2,1)} %bitcast.10, f32[64,2048]{1,0:T(8,128)} %state_exchange.1.incoming_ref, ...), custom_call_target="tpu_custom_call" | custom-call | tf_op jit(solution)/shard_map/outputs/pallas_call | solution.py:400
  65.7 11.9 %step_pool.1 = f32[16,128]{1,0:T(8,128)} custom-call(f32[8,128]{1,0:T(8,128)} %get-tuple-element.11.part_ref, s32[4,128]{1,0:T(4,128)} %bitcast.12, s32[4,128]{1,0:T(4,128)} %bitcast.13), custom_call_target="tpu_custom_call" | custom-call | tf_op jit(solution)/shard_map/step_pool/pallas_call | solution.py:417
  77.7 1.3 %slice_reduce_fusion = f32[16]{0:T(128)} fusion(f32[16,128]{1,0:T(8,128)} %step_pool.1), kind=kLoop, calls=%fused_computation | loop fusion | bytes 128 | tf_op jit(solution)/shard_map/slice | solution.py:429

commit v3 on v2

--- a/solution.py
+++ b/solution.py
@@ -56,7 +56,8 @@
     return jnp.where(inside, 1.0, 0.0).astype(BF16)
 
 
-def state_kernel(count, groups, lengths, x_ref, decay_ref, b_ref, enter_ref, before_ref, send_ref,
+def state_kernel(count, groups, lengths, x_ref, decay_ref, b_ref, c_ref, gain_ref, enter_ref,
+                 before_ref, send_ref, gram_ref, cum_ref, rows_ref, wide_gain_ref,
                  spread, state, factor):
     k = pl.program_id(0)
     heads, width = decay_ref.shape[0], x_ref.shape[1]
@@ -66,6 +67,8 @@
         spread[...] = spread_matrix(heads, width)
         state[...] = jnp.zeros_like(state)
         factor[...] = jnp.ones_like(factor)
+        wide_gain_ref[...] = jnp.dot(halves(jnp.broadcast_to(gain_ref[...], (16, heads))),
+                                     spread[...], preferred_element_type=F32)[:8]
 
     ends, passes = [], jnp.zeros((heads, LANES), F32)
     for sub in range(STATE_CHUNKS):
@@ -75,6 +78,12 @@
         trace = trace_at(lengths, first + iota((1, CHUNK), 1))
         last_trace = trace_at(lengths, jnp.full((1, 1), first + CHUNK - 1, jnp.int32))
         prev_trace = trace_at(lengths, jnp.full((1, 1), first - 1, jnp.int32))
+        rows_ref[:, tokens] = cum
+        cum_ref[tokens, :] = cum.T
+        trace_column = trace_at(lengths, first + iota((CHUNK, 1), 0))
+        keep = (iota((CHUNK, CHUNK), 0) >= iota((CHUNK, CHUNK), 1)) & (trace_column == trace)
+        gram = jnp.dot(c_ref[:, tokens].T, b_ref[:, tokens], preferred_element_type=F32)
+        gram_ref[tokens, :] = jnp.where(keep, gram, 0.0)
         end = cum[:, CHUNK - 1:]
         ends.append(jnp.exp2(end - cum) * jnp.where(trace == last_trace, 1.0, 0.0))
         through = jnp.exp2(end) * jnp.where(last_trace == prev_trace, 1.0, 0.0)
@@ -128,13 +137,38 @@
                         device_id_type=pl.DeviceIdType.MESH)
 
 
-def exchange_kernel(chips, groups, send_ref, out_ref, other, chip, arrived, answers, returned,
+def inside_chunk(k, x, gram_ref, cum_ref, rows_ref, gain_ref, held):
+    tokens = pl.ds(pl.multiple_of(k * CHUNK, CHUNK), CHUNK)
+    gram, cum, cum_rows = gram_ref[tokens, :], cum_ref[tokens, :], rows_ref[:, tokens]
+    low_half = iota((CHUNK, LANES), 1) < LANES // 2
+
+    def weight(h):
+        diff = jnp.minimum(cum[:, h:h + 1] - cum_rows[h:h + 1, :], 0.0)
+        return (gram * jnp.exp2(diff)).astype(BF16)
+
+    for pair in range(x.shape[1] // LANES):
+        columns = slice(pair * LANES, (pair + 1) * LANES)
+        x_pair = x[tokens, columns]
+        zero = jnp.zeros_like(x_pair)
+        both = jnp.concatenate(
+            [jnp.where(low_half, x_pair, zero), jnp.where(low_half, zero, x_pair)], axis=0)
+        weights = jnp.concatenate([weight(2 * pair), weight(2 * pair + 1)], axis=1)
+        held[tokens, columns] = (jnp.dot(weights, both, preferred_element_type=F32)
+                                 + gain_ref[:1, columns] * x_pair.astype(F32))
+
+
+def exchange_kernel(chips, groups, send_ref, gram_ref, cum_ref, rows_ref, gain_ref, x_ref,
+                    out_ref, inner_ref, x, held, load, store, other, chip, arrived, answers, returned,
                     theirs, last, pair_send, pair_recv, send_a, recv_a, send_b, recv_b):
     sec, dev = lax.axis_index("sec"), lax.axis_index("dev")
     per_sec = lax.axis_size("dev") // 2
     core = lax.rem(dev, 2)
     here = sec * per_sec + lax.div(dev, 2)
     early = core == 0
+    count = x.shape[0] // CHUNK
+    first_part = (count * 9) // 16
+    loading = pltpu.make_async_copy(x_ref, x, load.at[0])
+    loading.start()
     partner = (sec, dev + 1 - 2 * core)
     rows = answers.shape[1]
 
@@ -145,6 +179,14 @@
     each(1, chips, lambda off: greet(peer(off)[1]))
     greet(partner)
     pl.semaphore_wait(pltpu.get_barrier_semaphore(), chips)
+
+    def save(k):
+        tokens = pl.ds(pl.multiple_of(k * CHUNK, CHUNK), CHUNK)
+        return pltpu.make_async_copy(held.at[tokens], inner_ref.at[tokens], store.at[k])
+
+    def compute(k):
+        inside_chunk(k, x, gram_ref, cum_ref, rows_ref, gain_ref, held)
+        save(k).start()
 
     def to_partner(n, source, target):
         return pltpu.make_async_remote_copy(
@@ -184,6 +226,8 @@
     total, product = combine(here)
     arrived[here, :rows] = total
     arrived[here, rows:] = product
+    loading.wait()
+    each(0, first_part, compute)
     each(1, chips, lambda off: there(off).wait())
 
     def step(i, held):
@@ -194,6 +238,7 @@
     lax.fori_loop(0, chips, step, jnp.zeros(answers.shape[1:], F32))
     each(1, chips, lambda off: back(off).start())
     returned[here] = answers[here]
+    each(first_part, count, compute)
     each(1, chips, lambda off: back(off).wait())
 
     def split(p):
@@ -212,20 +257,18 @@
             pair, g = divmod(half * chips + p, groups)
             out_ref[g * rows:(g + 1) * rows, pair * LANES:(pair + 1) * LANES] = jnp.where(
                 core == half, returned[p], last[p])
-
-
-def output_kernel(count, lengths, x_ref, decay_ref, b_ref, c_ref, incoming_ref, enter_ref,
-                  before_ref, gain_ref, score_ref, steps_ref, y_ref, part_ref,
-                  spread, gain, starts):
+    each(0, count, lambda k: save(k).wait())
+
+
+def output_kernel(count, lengths, inner_ref, cum_ref, c_ref, incoming_ref, enter_ref,
+                  before_ref, score_ref, steps_ref, y_ref, part_ref, spread, starts):
     k = pl.program_id(0)
-    heads, width = decay_ref.shape[0], x_ref.shape[1]
+    heads, width = cum_ref.shape[1], inner_ref.shape[1]
     lines = steps_ref.shape[0]
 
     @pl.when(k == 0)
     def _():
         spread[...] = spread_matrix(heads, width)
-        gain[...] = jnp.dot(halves(jnp.broadcast_to(gain_ref[...], (16, heads))), spread[...],
-                            preferred_element_type=F32)[:8]
         sizes = steps_ref[...].astype(F32)
         upper = jnp.where(iota((LANES, LANES), 0) < iota((LANES, LANES), 1), 1.0, 0.0).astype(F32)
         inner = jnp.dot(sizes, upper, precision=lax.Precision.HIGHEST, preferred_element_type=F32)
@@ -236,49 +279,24 @@
             offset = offset + total[i:i + 1, :]
         part_ref[...] = jnp.zeros_like(part_ref)
 
+    quad = 2 * LANES
     for sub in range(OUTPUT_CHUNKS):
         first = (my_index() * count + k * OUTPUT_CHUNKS + sub) * CHUNK
         tokens = slice(sub * CHUNK, (sub + 1) * CHUNK)
-        cum_rows = running(decay_ref[:, tokens])
-        cum = cum_rows.T
         c = c_ref[:, tokens].T
         trace = trace_at(lengths, first + iota((CHUNK, 1), 0))
-        trace_row = trace_at(lengths, first + iota((1, CHUNK), 1))
         prev_trace = trace_at(lengths, jnp.full((1, 1), first - 1, jnp.int32))
-        keep = (iota((CHUNK, CHUNK), 0) >= iota((CHUNK, CHUNK), 1)) & (trace == trace_row)
-        gram = jnp.dot(c, b_ref[:, tokens], preferred_element_type=F32)
-        gram = jnp.where(keep, gram, 0.0)
-        c_kept = jnp.where(trace == prev_trace, c.astype(F32), 0.0).astype(BF16)
-        low_half = iota((CHUNK, LANES), 1) < LANES // 2
-        quad = 2 * LANES
-        scores = jnp.zeros((CHUNK, LANES), F32)
-
-        def weight(h):
-            here = jnp.broadcast_to(cum[:, h:h + 1], (CHUNK, CHUNK))
-            diff = jnp.minimum(here - cum_rows[h:h + 1, :], 0.0)
-            return here, (gram * jnp.exp2(diff)).astype(BF16)
-
+        carry = halves(jnp.exp2(cum_ref[tokens, :]) * jnp.where(trace == prev_trace, 1.0, 0.0))
+        scores = jnp.zeros((CHUNK, quad), F32)
         for q in range(width // quad):
-            wide = slice(q * quad, (q + 1) * quad)
-            full = (before_ref[sub, :1, wide] * incoming_ref[:, wide]
-                    + enter_ref[sub, :, wide].astype(F32)).astype(BF16)
-            inter = jnp.dot(c_kept, full, preferred_element_type=F32)
-            for half in range(2):
-                pair = 2 * q + half
-                columns = slice(pair * LANES, (pair + 1) * LANES)
-                x_pair = x_ref[tokens, columns]
-                zero = jnp.zeros_like(x_pair)
-                both = jnp.concatenate(
-                    [jnp.where(low_half, x_pair, zero), jnp.where(low_half, zero, x_pair)], axis=0)
-                here_a, weight_a = weight(2 * pair)
-                here_b, weight_b = weight(2 * pair + 1)
-                intra = jnp.dot(jnp.concatenate([weight_a, weight_b], axis=1), both,
-                                preferred_element_type=F32)
-                carry = jnp.exp2(jnp.where(low_half, here_a, here_b))
-                y = (intra + carry * inter[:, half * LANES:(half + 1) * LANES]
-                     + gain[:1, columns] * x_pair.astype(F32)).astype(BF16)
-                y_ref[tokens, columns] = y
-                scores = scores + y.astype(F32) * score_ref[:1, columns].astype(F32)
+            columns = slice(q * quad, (q + 1) * quad)
+            full = (before_ref[sub, :1, columns] * incoming_ref[:, columns]
+                    + enter_ref[sub, :, columns].astype(F32)).astype(BF16)
+            inter = jnp.dot(c, full, preferred_element_type=F32)
+            wide = jnp.dot(carry, spread[:, columns], preferred_element_type=F32)
+            y = (inner_ref[tokens, columns] + wide * inter).astype(BF16)
+            y_ref[tokens, columns] = y
+            scores = scores + y.astype(F32) * score_ref[:1, columns].astype(F32)
 
         score = jnp.sum(scores, axis=1, keepdims=True)
         places = (first + iota((CHUNK, 1), 0)).astype(F32)
@@ -348,8 +366,8 @@
     sections, across = lax.axis_size("sec"), lax.axis_size("dev")
     decay_rows, b_rows, c_rows = log_decay.T, b_input.T, c_input.T
 
-    def by_chunk(n):
-        return pl.BlockSpec((n * CHUNK, width), lambda k: (k, 0))
+    def by_chunk(n, columns=width):
+        return pl.BlockSpec((n * CHUNK, columns), lambda k: (k, 0))
 
     def by_row(n, lines):
         return pl.BlockSpec((lines, n * CHUNK), lambda k: (0, k))
@@ -360,21 +378,27 @@
     def fixed(*shape):
         return pl.BlockSpec(shape, lambda k: (0,) * len(shape))
 
-    enter, before, send = pl.pallas_call(
+    enter, before, send, gram, cum, cum_rows, gain = pl.pallas_call(
         functools.partial(state_kernel, count, groups),
         grid=(count // STATE_CHUNKS,),
         in_specs=[scalar, by_chunk(STATE_CHUNKS), by_row(STATE_CHUNKS, heads),
-                  by_row(STATE_CHUNKS, state_size)],
+                  by_row(STATE_CHUNKS, state_size), by_row(STATE_CHUNKS, state_size),
+                  fixed(1, heads)],
         out_specs=[by_chunk3(STATE_CHUNKS, state_size, width), by_chunk3(STATE_CHUNKS, 8, width),
-                   fixed(devices, depth + 8, LANES)],
+                   fixed(devices, depth + 8, LANES), by_chunk(STATE_CHUNKS, CHUNK),
+                   by_chunk(STATE_CHUNKS, heads), by_row(STATE_CHUNKS, heads), fixed(8, width)],
         out_shape=[jax.ShapeDtypeStruct((count, state_size, width), BF16),
                    jax.ShapeDtypeStruct((count, 8, width), F32),
-                   jax.ShapeDtypeStruct((devices, depth + 8, LANES), F32)],
+                   jax.ShapeDtypeStruct((devices, depth + 8, LANES), F32),
+                   jax.ShapeDtypeStruct((rows, CHUNK), F32),
+                   jax.ShapeDtypeStruct((rows, heads), F32),
+                   jax.ShapeDtypeStruct((heads, rows), F32),
+                   jax.ShapeDtypeStruct((8, width), F32)],
         scratch_shapes=[pltpu.VMEM((2 * heads, width), BF16), pltpu.VMEM((state_size, width), F32),
                         pltpu.VMEM((8, width), F32)],
         compiler_params=pltpu.CompilerParams(vmem_limit_bytes=VMEM_BYTES),
         name="chunk_states",
-    )(trace_lengths, x_input, decay_rows, b_rows)
+    )(trace_lengths, x_input, decay_rows, b_rows, c_rows, skip_gain.reshape(1, heads))
 
     def sems(n):
         return pltpu.SemaphoreType.DMA((n,))
@@ -382,37 +406,38 @@
     def blocks(lines):
         return pltpu.VMEM((chips, lines, LANES), F32)
 
-    incoming = pl.pallas_call(
+    incoming, inner = pl.pallas_call(
         functools.partial(exchange_kernel, chips, groups),
-        in_specs=[whole],
-        out_specs=whole,
-        out_shape=jax.ShapeDtypeStruct((state_size, width), F32),
-        scratch_shapes=[blocks(depth + 8), blocks(depth + 8), blocks(depth + 8), blocks(depth),
+        in_specs=[whole, whole, whole, whole, whole, pl.BlockSpec(memory_space=pl.ANY)],
+        out_specs=[whole, pl.BlockSpec(memory_space=pl.ANY)],
+        out_shape=[jax.ShapeDtypeStruct((state_size, width), F32),
+                   jax.ShapeDtypeStruct((rows, width), F32)],
+        scratch_shapes=[pltpu.VMEM((rows, width), BF16), pltpu.VMEM((rows, width), F32),
+                        sems(1), sems(count), blocks(depth + 8), blocks(depth + 8), blocks(depth + 8), blocks(depth),
                         blocks(depth), blocks(depth), blocks(depth), sems(2), sems(2),
                         sems(chips), sems(chips), sems(chips), sems(chips)],
         compiler_params=pltpu.CompilerParams(collective_id=0, has_side_effects=True,
                                              vmem_limit_bytes=VMEM_BYTES),
         name="state_exchange",
-    )(send)
+    )(send, gram, cum, cum_rows, gain, x_input)
 
     lines8 = max(8, lines)
     steps_rows = step_lengths.reshape(lines, LANES)
     y_output, part = pl.pallas_call(
         functools.partial(output_kernel, count),
         grid=(count // OUTPUT_CHUNKS,),
-        in_specs=[scalar, by_chunk(OUTPUT_CHUNKS), by_row(OUTPUT_CHUNKS, heads),
-                  by_row(OUTPUT_CHUNKS, state_size), by_row(OUTPUT_CHUNKS, state_size),
-                  fixed(state_size, width), by_chunk3(OUTPUT_CHUNKS, state_size, width),
-                  by_chunk3(OUTPUT_CHUNKS, 8, width), fixed(1, heads), fixed(1, width), fixed(lines, LANES)],
+        in_specs=[scalar, by_chunk(OUTPUT_CHUNKS), by_chunk(OUTPUT_CHUNKS, heads),
+                  by_row(OUTPUT_CHUNKS, state_size), fixed(state_size, width),
+                  by_chunk3(OUTPUT_CHUNKS, state_size, width), by_chunk3(OUTPUT_CHUNKS, 8, width),
+                  fixed(1, width), fixed(lines, LANES)],
         out_specs=[by_chunk(OUTPUT_CHUNKS), fixed(lines8, LANES)],
         out_shape=[jax.ShapeDtypeStruct((rows, width), BF16),
                    jax.ShapeDtypeStruct((lines8, LANES), F32)],
-        scratch_shapes=[pltpu.VMEM((2 * heads, width), BF16), pltpu.VMEM((8, width), F32),
-                        pltpu.VMEM((lines8, LANES), F32)],
+        scratch_shapes=[pltpu.VMEM((2 * heads, width), BF16), pltpu.VMEM((lines8, LANES), F32)],
         compiler_params=pltpu.CompilerParams(vmem_limit_bytes=VMEM_BYTES),
         name="outputs",
-    )(trace_lengths, x_input, decay_rows, b_rows, c_rows, incoming, enter, before,
-      skip_gain.reshape(1, heads), score_weight.reshape(1, width), steps_rows)
+    )(trace_lengths, inner, cum, c_rows, incoming, enter, before,
+      score_weight.reshape(1, width), steps_rows)
 
     pooled = pl.pallas_call(
         functools.partial(pool_kernel, owned),

time: 79.3 us -> 71.1 us (0.90)
  Pallas kernels: 75.7 us -> 67.4 us
    pallas_call x1, Pallas kernels: 26.1 us -> 15.8 us  [shards(): pl.pallas_call(functools.partial(output_kernel, count), grid=(count // OU...]
    pallas_call x1, Pallas kernels: 10.2 us -> 11.3 us  [shards(): pl.pallas_call(functools.partial(state_kernel, count, groups), grid=(coun...]
    pallas_call x1, Pallas kernels: 27.4 us -> 28.3 us  [shards(): pl.pallas_call(functools.partial(exchange_kernel, chips, groups), in_spec...]
where the time goes in v3:
time: 71.1 us; the launch traced here: 70.7 us
  Pallas kernels  67.4 us (95%)
  local copies, waits for them, and re-layouts  2.61 us (4%)
    pallas_call x1, Pallas kernels, shards(): pl.pallas_call(functools.partial(exchange_kernel, chips, groups), in_spec...  28.3 us
    pallas_call x1, Pallas kernels, shards(): pl.pallas_call(functools.partial(output_kernel, count), grid=(count // OU...  15.8 us
    pallas_call x1, Pallas kernels, shards(): pl.pallas_call(functools.partial(pool_kernel, owned), in_specs=[whole, wh...  12 us
    pallas_call x1, Pallas kernels, shards(): pl.pallas_call(functools.partial(state_kernel, count, groups), grid=(coun...  11.3 us

profile of v3, /device:TPU:0, one launch (start us, length us, event | category | flops | bytes accessed | tf_op | source)
XLA Modules:
  0.0 70.7 jit_solution(5417005448639893735)
XLA Ops:
  0.6 1.3 %reshape.17.score_ref = bf16[1,2048]{1,0:T(2,128)(2,1)} reshape(bf16[2048]{0:T(1024)(128)(2,1)} %param.14) | data formatting | bytes 8192 | tf_op jit(solution)/shard_map/reshape | solution.py:440
  1.9 11.3 %chunk_states.1 = (bf16[16,64,2048]{2,1,0:T(8,128)(2,1)}, f32[16,8,2048]{2,1,0:T(8,128)}, f32[32,40,128]{2,1,0:T(8,128)}, f32[2048,128]{1,0:T(8,128)}, f32[2048,...) custom-call(s32[4]{0:T(128)} %lengths.3, bf16[2048,2048]{1,0:T(8,128)(2,1)} %x_ref.3, f32[32,2048]{1,0:T(8,128)} %bitcast.8, ...), custom_call_target="tpu_custom_call" | custom-call | tf_op jit(solution)/shard_map/chunk_states/pallas_call | solution.py:381
  13.3 28.3 %state_exchange.1 = (f32[64,2048]{1,0:T(8,128)}, f32[2048,2048]{1,0:T(8,128)}) custom-call(f32[32,40,128]{2,1,0:T(8,128)} %get-tuple-element.13.send_ref, f32[2048,128]{1,0:T(8,128)} %get-tuple-element.14.gram_ref, f32[2048,32]{1,0:T(8,128)} %get-tuple-element.15.cum_ref, f32[32,2048]{1,0:T(8,128)} %get-tuple-element.16.rows_ref, ...), custom_call_target="tpu_custom_call" | custom-call | tf_op jit(solution)/shard_map/state_exchange/pallas_call | solution.py:409
  41.6 15.8 %outputs.1 = (bf16[2048,2048]{1,0:T(8,128)(2,1)}, f32[8,128]{1,0:T(8,128)}) custom-call(s32[4]{0:T(128)} %lengths.3, f32[2048,2048]{1,0:T(8,128)} %get-tuple-element.18.inner_ref, f32[2048,32]{1,0:T(8,128)} %get-tuple-element.15.cum_ref, bf16[64,2048]{1,0:T(8,128)(2,1)} %bitcast.7, f32[64,2048]{1,0:T(8,128)} %get-tuple-element.19.incoming_ref, ...), custom_call_target="tpu_custom_call" | custom-call | tf_op jit(solution)/shard_map/outputs/pallas_call | solution.py:426
  57.3 12.0 %step_pool.1 = f32[16,128]{1,0:T(8,128)} custom-call(f32[8,128]{1,0:T(8,128)} %get-tuple-element.23.part_ref, s32[4,128]{1,0:T(4,128)} %bitcast.11, s32[4,128]{1,0:T(4,128)} %bitcast.12), custom_call_target="tpu_custom_call" | custom-call | tf_op jit(solution)/shard_map/step_pool/pallas_call | solution.py:442
  69.4 1.3 %slice_reduce_fusion = f32[16]{0:T(128)} fusion(f32[16,128]{1,0:T(8,128)} %step_pool.1), kind=kLoop, calls=%fused_computation | loop fusion | bytes 128 | tf_op jit(solution)/shard_map/slice | solution.py:454
